TPU v7x, 512 devices: a whole 4x4x16 slice. The times are simulated.
512 devices in a mesh: table: 32 (over x, z_lo, core), replica: 16 (over y, z_hi).
Axes of the slice: x: 4, y: 4, z: 16 (z_hi: 4, z_lo: 4; z = z_hi * 4 + z_lo), core: 2. Of those that a mesh axis runs over, the one named last changes fastest.
Arguments:
- top_input: bfloat16 [16384, 2048], P('replica'), may hold values from -6 to 6
- cotangent: bfloat16 [2048, 16384], P('table', 'replica'), may hold values from -0.25 to 0.25
- w_first: bfloat16 [2048, 2048], P('table'), may hold values from -0.125 to 0.125
- w_second: bfloat16 [2048, 2048], P('table'), may hold values from -0.125 to 0.125
- sectioned_rows: float32 [16, 128, 256, 256], P('replica', 'table'), may hold values from -6 to 6
- projection: bfloat16 [128, 256, 256], P('table'), may hold values from -0.375 to 0.375
- bag_ids: int32 [16, 256, 128, 16], P('replica', None, 'table'), may hold values from 0 to 255
- bag_lengths: int32 [16, 256, 128], P('replica', None, 'table'), may hold values from 1 to 16
- table_width: int32 [128], P('table'), may hold values from 32 to 256, as said below
Outputs:
- grad_first: bfloat16 [2048, 2048], P('table')
- grad_second: bfloat16 [2048, 2048], P('table')
- pooled_rows: bfloat16 [16, 256, 32768], P('replica', 'table')
Inputs may be any that keep to these rules, and one draw needn't show every extreme that they name: `table_width`: each table's width is 256 // 8 times 1, 2, 4 or 8.
All inputs are finite; a program needn't handle non-finite values.
Results may differ from a plain program's by a relative error of at most 0.0051.
Values may be sent and summed in bfloat16 or wider, within the bound.
A program may use at most 64 MiB of HBM per device.

v0:
```python
import jax
import jax.numpy as jnp
from jax import lax
from jax.sharding import PartitionSpec as P


def pool_tables(sectioned_rows, projection, bag_ids, bag_lengths, table_width):
    identities = bag_ids[0]
    lengths_here = bag_lengths[0]
    sectioned_here = sectioned_rows[0]
    bag_slots = lax.broadcasted_iota(jnp.int32, identities.shape, 2)
    present = bag_slots < lengths_here[:, :, None]
    row_numbers = lax.broadcasted_iota(jnp.int32, (1, 1, 1, sectioned_here.shape[1]), 3)
    matches = jnp.logical_and(present[..., None], identities[..., None] == row_numbers)
    counts = jnp.sum(matches.astype(jnp.float32), axis=2)
    pooled = jnp.einsum(
        "str,trw->stw",
        counts,
        sectioned_here,
        precision=lax.Precision.HIGHEST,
        preferred_element_type=jnp.float32,
    )
    columns = lax.broadcasted_iota(jnp.int32, (1, 1, sectioned_here.shape[2]), 2)
    masked = jnp.where(columns < table_width[None, :, None], pooled, 0.0).astype(jnp.bfloat16)
    projected = jnp.einsum(
        "stw,twe->ste", masked, projection, preferred_element_type=jnp.float32
    ).astype(jnp.bfloat16)
    flattened = projected.reshape(projected.shape[0], -1)
    received = lax.all_to_all(flattened, "table", split_axis=0, concat_axis=1, tiled=True)
    return received[None]


def top_gradients(top_input, cotangent, w_first, w_second):
    pre_act = lax.dot_general(
        w_first, top_input, (((1,), (1,)), ((), ())), preferred_element_type=jnp.float32
    )
    logistic = jax.nn.sigmoid(pre_act)
    hidden = (pre_act * logistic).astype(jnp.bfloat16)
    slopes = logistic * (1.0 + pre_act * (1.0 - logistic))
    shard_rows = lax.all_gather(cotangent, "table", axis=0, tiled=True)
    d_hidden = jnp.dot(w_second, shard_rows, preferred_element_type=jnp.float32)
    column_block = lax.dot_general(
        hidden, shard_rows, (((1,), (1,)), ((), ())), preferred_element_type=jnp.float32
    )
    second_sum = column_block
    d_hidden, second_sum = (d_hidden, second_sum)
    d_pre = (d_hidden * slopes).astype(jnp.bfloat16)
    first_sum = jnp.dot(d_pre, top_input, preferred_element_type=jnp.float32)
    first_total, second_total = lax.psum((first_sum, second_sum), "replica")
    return (first_total.astype(jnp.bfloat16), second_total.astype(jnp.bfloat16))


def shards(
    top_input,
    cotangent,
    w_first,
    w_second,
    sectioned_rows,
    projection,
    bag_ids,
    bag_lengths,
    table_width,
):
    grad_first, grad_second = top_gradients(top_input, cotangent, w_first, w_second)
    pooled_rows = pool_tables(sectioned_rows, projection, bag_ids, bag_lengths, table_width)
    return (grad_first, grad_second, pooled_rows)


def solution(mesh):
    placed = (
        P("replica", None),
        P("table", "replica"),
        P("table", None),
        P("table", None),
        P("replica", "table", None, None),
        P("table", None, None),
        P("replica", None, "table", None),
        P("replica", None, "table"),
        P("table"),
    )
    return jax.shard_map(
        shards,
        mesh=mesh,
        in_specs=placed,
        out_specs=(P("table", None), P("table", None), P("replica", "table", None)),
        check_vma=False,
    )
```

profile of v0, /device:TPU:122, one launch (start us, length us, event | category | flops | bytes accessed | tf_op | source)
XLA Modules:
  0.0 259.7 jit_solution(112769670518205922)
XLA Ops:
  7.2 0.0 copy-start
  7.2 0.0 copy-start.1
  7.2 0.0 all-gather.2.cloned.1.call-start
  7.2 0.7 all-gather.2.cloned.1.call-update
  7.9 1.1 copy.18
  9.0 0.8 copy.17
  9.8 0.7 iota_compare_fusion.2
  10.6 0.3 iota_compare_fusion.1
  10.9 0.0 copy-start.2
  10.9 8.9 %convert_reduce_fusion = f32[256,4,256]{2,1,0:T(4,128)S(1)} fusion(s32[256,4,16]{2,1,0:T(4,128)S(1)} %copy.18, pred[256,4,16]{2,1,0:T(4,128)(4,1)S(1)} %iota_compare_fusion.1), kind=kLoop, calls=%fused_computation | loop fusion | flops 16515072 | bytes 1130496 | tf_op jit(solution)/shard_map/reduce_sum | solution.py:15
  19.8 0.0 copy-done
  19.8 1.2 fusion.2
  21.0 0.0 copy-done.1
  21.0 0.3 fusion.3
  21.4 0.0 copy-start.3
  21.4 0.4 copy.20
  21.8 1.2 all_to_all.12
  22.9 7.7 %all-to-all-start = ((bf16[32,8,1024]{2,1,0:T(8,128)(2,1)}), bf16[32,8,1024]{2,1,0:T(8,128)(2,1)S(1)}, u32[]{:S(2)}, u32[]{:S(2)}) async-start(bf16[32,8,1024]{2,1,0:T(8,128)(2,1)} %all_to_all.12), calls=%async_computation | async-start | bytes 1048576 | tf_op jit(solution)/shard_map/all_to_all | solution.py:29
  30.7 0.0 copy-done.2
  30.7 3.6 %fusion.17 = f32[64,1024]{1,0:T(8,128)S(1)} fusion(bf16[64,2048]{1,0:T(8,128)(2,1)S(1)} %copy-done.2, bf16[1024,2048]{1,0:T(8,128)(2,1)} %param.9), kind=kOutput, calls=%fused_computation.26 | convolution fusion | flops 268435456 | bytes 4718592 | tf_op jit(solution)/shard_map/dot_general | solution.py:34
  34.2 13.3 %all-to-all-done = bf16[32,8,1024]{2,1,0:T(8,128)(2,1)S(1)} async-done(((bf16[32,8,1024]{2,1,0:T(8,128)(2,1)}), bf16[32,8,1024]{2,1,0:T(8,128)(2,1)S(1)}, u32[]{:S(2)}, u32[]{:S(2)}) %all-to-all-start) | async-done | bytes 524320 | tf_op jit(solution)/shard_map/all_to_all | solution.py:29
  47.5 36.2 %all-gather.2.cloned.1.call-done = bf16[2048,1024]{1,0:T(8,128)(2,1)} async-done(((bf16[64,1024]{1,0:T(8,128)(2,1)}), bf16[2048,1024]{1,0:T(8,128)(2,1)}) %all-gather.2.cloned.1.call-update) | async-done | bytes 4194320 | tf_op jit(solution)/shard_map/all_gather | solution.py:40
  83.7 0.0 copy-done.3
  83.7 5.1 %fusion.5 = f32[64,2048]{1,0:T(8,128)S(1)} fusion(bf16[1024,2048]{1,0:T(8,128)(2,1)} %param.9, bf16[64,2048]{1,0:T(8,128)(2,1)S(1)} %copy-done.3, bf16[2048,1024]{1,0:T(8,128)(2,1)} %all-gather.2.cloned.1.call-done, f32[64,1024]{1,0:T(8,128)S(1)} %fusion.17), kind=kOutput, calls=%fused_computation.10 | convolution fusion | flops 537460736 | bytes 9437184 | tf_op jit(solution)/shard_map/dot_general | solution.py:48
  88.8 3.6 %fusion.12 = f32[64,2048]{1,0:T(8,128)S(1)} fusion(bf16[2048,1024]{1,0:T(8,128)(2,1)} %all-gather.2.cloned.1.call-done, f32[64,1024]{1,0:T(8,128)S(1)} %fusion.17), kind=kOutput, calls=%fused_computation.20 | convolution fusion | flops 268763136 | bytes 4980736 | tf_op jit(solution)/shard_map/dot_general | solution.py:42
  92.4 159.7 %all-reduce.2 = (bf16[64,2048]{1,0:T(8,128)(2,1)}, bf16[64,2048]{1,0:T(8,128)(2,1)}) all-reduce(f32[64,2048]{1,0:T(8,128)S(1)} %fusion.5, f32[64,2048]{1,0:T(8,128)S(1)} %fusion.12), channel_id=1, replica_groups=mesh['table'=32,'replica'=16] {'replica'}, use_global_device_ids=true, to_apply=%region_0.0 | all-reduce | flops 262144 | bytes 1572864 | tf_op jit(solution)/shard_map/psum | solution.py:49
  252.1 0.8 copy.28
Async XLA Ops:
  7.2 12.6 %copy-start = (f32[1,4,256,256]{3,2,1,0:T(8,128)S(1)}, f32[1,4,256,256]{3,2,1,0:T(8,128)}, u32[]{:S(2)}) copy-start(f32[1,4,256,256]{3,2,1,0:T(8,128)} %param.13) | copy-start | bytes 3145732
  7.2 13.9 %copy-start.1 = (bf16[4,256,256]{2,1,0:T(8,128)(2,1)S(1)}, bf16[4,256,256]{2,1,0:T(8,128)(2,1)}, u32[]{:S(2)}) copy-start(bf16[4,256,256]{2,1,0:T(8,128)(2,1)} %param.14) | copy-start | bytes 1572868
  7.2 76.5 %all-gather.2.cloned.1.call-start = ((), (), s32[]{:S(2)}) async-start(), calls=%async_computation.1 | async-start | bytes 4325376 | tf_op jit(solution)/shard_map/all_gather | solution.py:40
  10.9 19.8 %copy-start.2 = (bf16[64,2048]{1,0:T(8,128)(2,1)S(1)}, bf16[64,2048]{1,0:T(8,128)(2,1)}, u32[]{:S(2)}) copy-start(bf16[64,2048]{1,0:T(8,128)(2,1)} %param.11) | copy-start | bytes 786436
  21.4 62.3 %copy-start.3 = (bf16[64,2048]{1,0:T(8,128)(2,1)S(1)}, bf16[64,2048]{1,0:T(8,128)(2,1)}, u32[]{:S(2)}) copy-start(bf16[64,2048]{1,0:T(8,128)(2,1)} %param.12) | copy-start | bytes 786436
  22.9 24.6 %all-to-all-start = ((bf16[32,8,1024]{2,1,0:T(8,128)(2,1)}), bf16[32,8,1024]{2,1,0:T(8,128)(2,1)S(1)}, u32[]{:S(2)}, u32[]{:S(2)}) async-start(bf16[32,8,1024]{2,1,0:T(8,128)(2,1)} %all_to_all.12), calls=%async_computation | async-start | bytes 1048576 | tf_op jit(solution)/shard_map/all_to_all | solution.py:29
Sparse Core Ops, SparseCore 0:
  10.2 73.4 all-gather.1
where the time goes:
time: 260 us
  blocking collectives  160 us (62%)
  waiting for transfers between devices  50.1 us (19%)
  between operations  14.2 us (5%)
  matrix products  13.8 us (5%)
  other arithmetic  9.95 us (4%)
  starting transfers between devices  7.73 us (3%)
  local copies, waits for them, and re-layouts  4.27 us (2%)
    psum x1, blocking collectives, top_gradients(): first_total, second_total = lax.psum((first_sum, second_sum), 'replica')  160 us
    all_gather x1, waiting for transfers between devices, top_gradients(): shard_rows = lax.all_gather(cotangent, 'table', axis=0, tiled=True)  36.2 us
    all_to_all x1, waiting for transfers between devices, pool_tables(): lax.all_to_all(flattened, 'table', split_axis=0, concat_axis=1, tiled=True)  13.3 us
    reduce_sum x1, other arithmetic, pool_tables(): counts = jnp.sum(matches.astype(jnp.float32), axis=2)  8.88 us
    all_to_all x1, starting transfers between devices, pool_tables(): lax.all_to_all(flattened, 'table', split_axis=0, concat_axis=1, tiled=True)  7.69 us
  transfers between devices with their start and end apart: 2, of which 2 were waited for; matrix products, arithmetic and copies ran while one was open for 7% of the time, Pallas kernels for 0%

commit v1 on v0

v1 whole, which is shorter than its diff:
```python
import jax
import jax.numpy as jnp
from jax import lax
from jax.experimental import pallas as pl
from jax.experimental.pallas import tpu as pltpu
from jax.sharding import PartitionSpec as P

MESH = pl.DeviceIdType.MESH
F32 = jnp.float32
BF16 = jnp.bfloat16

HIDDEN = 64
ROWS = 1024
FEATS = 2048
BLOCK = 64
PIECE = 512
PIECES = 4
SHARE = 16
PEERS = 32
TABLES = 4
LANES = 256

Z_AT = 0
X_AT = Z_AT + 3
HALF_AT = X_AT + 8
CORE_AT = HALF_AT + 8
PIECE_AT = CORE_AT + 16
SPREAD_AT = PIECE_AT + 9 * 2 * PIECES
COPIES = SPREAD_AT + PEERS - 1


def wrap(value, size):
    return lax.rem(value + size, size)


def kernel(
    widths,
    top_hbm,
    cot_hbm,
    first_hbm,
    second_hbm,
    rows_hbm,
    proj_hbm,
    ids_hbm,
    lens_hbm,
    out_first,
    out_second,
    out_pooled,
    top,
    cot,
    first,
    second,
    rows,
    proj,
    ids,
    lens,
    hidden,
    slope,
    d_hidden,
    part,
    part_b,
    y_in,
    z_in,
    result,
    spread,
    arrived,
    local_sem,
    send_sem,
    recv_sem,
):
    table = lax.axis_index("table")
    replica = lax.axis_index("replica")
    x = lax.div(table, 8)
    z = lax.rem(lax.div(table, 2), 4)
    c = lax.rem(table, 2)
    y = lax.div(replica, 4)
    zh = lax.rem(replica, 4)

    def table_of(x_, z_, c_):
        return x_ * 8 + z_ * 2 + c_

    def block(x_, z_, c_, half=None):
        start = table_of(x_, z_, c_) * BLOCK
        if half is None:
            return cot.at[pl.ds(pl.multiple_of(start, BLOCK), BLOCK)]
        size = BLOCK // 2
        return cot.at[pl.ds(pl.multiple_of(start + half * size, size), size)]

    def remote(number, src, dst, to_table, to_replica):
        return pltpu.make_async_remote_copy(
            src_ref=src,
            dst_ref=dst,
            send_sem=send_sem.at[number],
            recv_sem=recv_sem.at[number],
            device_id=(to_table, to_replica),
            device_id_type=MESH,
        )

    sent = []

    def send(number, src, dst, to_table, to_replica):
        copy = remote(number, src, dst, to_table, to_replica)
        copy.start()
        sent.append(copy)

    def receive(number, dst):
        remote(number, dst, dst, table, replica).wait_recv()

    def local(number, src, dst):
        copy = pltpu.make_async_copy(src, dst, local_sem.at[number])
        copy.start()
        return copy

    mine = block(x, z, c)
    load_cot = local(0, cot_hbm, mine)
    load_first = local(1, first_hbm, first)
    load_top = local(2, top_hbm, top)
    load_ids = local(3, ids_hbm, ids)
    load_lens = local(4, lens_hbm, lens)
    load_rows = local(5, rows_hbm, rows)
    load_proj = local(6, proj_hbm, proj)
    load_second = local(7, second_hbm, second)

    barrier = pltpu.get_barrier_semaphore()
    for k in range(1, PEERS):
        pl.semaphore_signal(
            barrier, inc=1, device_id=(wrap(table + k, PEERS), replica), device_id_type=MESH
        )
    for k in range(1, 4):
        pl.semaphore_signal(
            barrier, inc=1, device_id=(table, wrap(y + k, 4) * 4 + zh), device_id_type=MESH
        )
        pl.semaphore_signal(
            barrier, inc=1, device_id=(table, y * 4 + wrap(zh + k, 4)), device_id_type=MESH
        )
    load_cot.wait()
    pl.semaphore_wait(barrier, PEERS - 1 + 6)

    x_up, x_down, x_far = wrap(x + 1, 4), wrap(x - 1, 4), wrap(x + 2, 4)
    columns = (x, x_up, x_down, x_far)

    def to_core(which, j):
        ref = block(columns[which], wrap(z + j, 4), c)
        send(CORE_AT + which * 4 + j, ref, ref, table_of(x, z, 1 - c), replica)

    def from_core(which):
        for j in range(4):
            ref = block(columns[which], wrap(z + j, 4), 1 - c)
            receive(CORE_AT + which * 4 + j, ref)

    def to_x(j):
        ref = block(x, wrap(z + j, 4), c)
        send(X_AT + j, ref, ref, table_of(x_up, z, c), replica)
        send(X_AT + 4 + j, ref, ref, table_of(x_down, z, c), replica)

    def from_x(j):
        zj = wrap(z + j, 4)
        receive(X_AT + j, block(x_down, zj, c))
        ref = block(x_down, zj, c, 0)
        send(HALF_AT + j, ref, ref, table_of(x_up, z, c), replica)
        receive(X_AT + 4 + j, block(x_up, zj, c))
        ref = block(x_up, zj, c, 1)
        send(HALF_AT + 4 + j, ref, ref, table_of(x_down, z, c), replica)
        to_core(2, j)
        to_core(1, j)

    def from_far(j):
        zj = wrap(z + j, 4)
        receive(HALF_AT + j, block(x_far, zj, c, 0))
        receive(HALF_AT + 4 + j, block(x_far, zj, c, 1))
        to_core(3, j)

    for k in (1, 3, 2):
        send(Z_AT + k - 1, mine, mine, table_of(x, wrap(z + k, 4), c), replica)
    to_x(0)
    to_core(0, 0)

    load_first.wait()
    load_top.wait()

    def forward(step, carry):
        at = pl.ds(pl.multiple_of(step * 256, 256), 256)
        pre = lax.dot_general(
            first[...], top[at, :], (((1,), (1,)), ((), ())), preferred_element_type=F32
        )
        s = 1.0 / (1.0 + jnp.exp(-pre))
        hidden[:, at] = (pre * s).astype(BF16)
        slope[:, at] = s * (1.0 + pre * (1.0 - s))
        return carry

    lax.fori_loop(0, 4, forward, 0)

    load_ids.wait()
    load_lens.wait()
    load_rows.wait()
    load_proj.wait()

    def pool(t):
        slots = lax.broadcasted_iota(jnp.int32, (16, LANES), 0)
        live = jnp.where(slots < lens[t : t + 1, :], ids[t], -1)
        numbers = lax.broadcasted_iota(jnp.int32, (LANES, LANES), 0)
        counts = jnp.zeros((LANES, LANES), F32)
        for k in range(16):
            counts = counts + jnp.where(live[k : k + 1, :] == numbers, 1.0, 0.0)
        counts = counts.T.astype(BF16)
        whole = rows[t]
        high = whole.astype(BF16)
        rest = whole - high.astype(F32)
        middle = rest.astype(BF16)
        low = (rest - middle.astype(F32)).astype(BF16)
        pooled = jnp.dot(counts, low, preferred_element_type=F32)
        pooled = pooled + jnp.dot(counts, middle, preferred_element_type=F32)
        pooled = pooled + jnp.dot(counts, high, preferred_element_type=F32)
        lanes = lax.broadcasted_iota(jnp.int32, (LANES, LANES), 1)
        kept = jnp.where(lanes < widths[t], pooled, 0.0).astype(BF16)
        return jnp.dot(kept, proj[t], preferred_element_type=F32)

    def pool_pair(t):
        upper = pool(t).reshape(PEERS, 8, LANES)
        lower = pool(t + 2).reshape(PEERS, 8, LANES)
        spread[:, :, t * LANES : (t + 1) * LANES] = jnp.concatenate([upper, lower], 1).astype(BF16)

    def column_step(which):
        at = pl.ds(pl.multiple_of(columns[which] * PIECE, PIECE), PIECE)
        there = cot[at, :]
        product = jnp.dot(second[:, at], there, preferred_element_type=F32)
        if which == 0:
            d_hidden[...] = product
        else:
            d_hidden[...] += product
        share_out(
            which,
            lax.dot_general(
                hidden[...], there, (((1,), (1,)), ((), ())), preferred_element_type=F32
            ),
        )

    def piece_at(p):
        if p < PIECES:
            return 1, pl.ds(pl.multiple_of(columns[p] * PIECE, PIECE), PIECE)
        return 0, pl.ds((p - PIECES) * PIECE, PIECE)

    def share(y_):
        return pl.ds(pl.multiple_of(y_ * SHARE, SHARE), SHARE)

    def share_out(p, value):
        part[p] = value
        part_b[p] = value.astype(BF16)
        for k in range(1, 4):
            to = wrap(y + k, 4)
            send(PIECE_AT + 9 * p + k - 1, part_b.at[p, share(to)], y_in.at[p, k - 1], table, to * 4 + zh)

    def exchange(p):
        total = part[p, share(y), :]
        for k in range(1, 4):
            receive(PIECE_AT + 9 * p + k - 1, y_in.at[p, k - 1])
            total = total + y_in[p, k - 1].astype(F32)
        z_in[p, zh] = total.astype(BF16)
        for k in range(1, 4):
            send(
                PIECE_AT + 9 * p + 3 + k - 1,
                z_in.at[p, zh],
                z_in.at[p, zh],
                table,
                y * 4 + wrap(zh + k, 4),
            )

    def finish(p):
        for k in (1, 3, 2):
            receive(PIECE_AT + 9 * p + 3 + k - 1, z_in.at[p, wrap(zh - k, 4)])
        total = z_in[p, 0].astype(F32)
        for k in range(1, 4):
            total = total + z_in[p, k].astype(F32)
        which, at = piece_at(p)
        result[which, share(y), at] = total.astype(BF16)
        ref = result.at[which, share(y), at]
        for k in range(1, 4):
            send(PIECE_AT + 9 * p + 6 + k - 1, ref, ref, table, wrap(y + k, 4) * 4 + zh)

    def collect(p):
        which, at = piece_at(p)
        for k in range(1, 4):
            receive(PIECE_AT + 9 * p + 6 + k - 1, result.at[which, share(wrap(y - k, 4)), at])

    from_x(0)
    pool_pair(0)
    for k in (1, 3, 2):
        receive(Z_AT + k - 1, block(x, wrap(z - k, 4), c))
        to_x(4 - k)
        to_core(0, 4 - k)
    pool_pair(1)
    load_second.wait()
    from_core(0)
    column_step(0)
    for j in (3, 1, 2):
        from_x(j)
    for k in range(1, PEERS):
        to = wrap(table + k, PEERS)
        send(SPREAD_AT + k - 1, spread.at[to], arrived.at[table], to, replica)
    arrived[table] = spread[table]
    exchange(0)
    from_core(1)
    column_step(1)
    from_core(2)
    column_step(2)
    for j in (0, 3, 1, 2):
        from_far(j)
    exchange(1)
    exchange(2)
    from_core(3)
    column_step(3)
    d_pre = (d_hidden[...] * slope[...]).astype(BF16)
    for q in range(PIECES):
        share_out(
            PIECES + q,
            jnp.dot(d_pre, top[:, q * PIECE : (q + 1) * PIECE], preferred_element_type=F32),
        )
    for p in range(3, 2 * PIECES):
        exchange(p)
    for p in range(2 * PIECES):
        finish(p)
    for k in range(1, PEERS):
        receive(SPREAD_AT + k - 1, arrived.at[wrap(table - k, PEERS)])

    def place(j, carry):
        value = arrived[j].astype(F32)
        start = pl.multiple_of(j * 1024, 1024)
        out_pooled[0, :, pl.ds(start, 512)] = value[:8].astype(BF16)
        out_pooled[0, :, pl.ds(start + 512, 512)] = value[8:].astype(BF16)
        return carry

    lax.fori_loop(0, PEERS, place, 0)
    for p in range(2 * PIECES):
        collect(p)
    out_first[...] = result[0]
    out_second[...] = result[1]
    for copy in sent:
        copy.wait_send()


def shards(
    top_input,
    cotangent,
    w_first,
    w_second,
    sectioned_rows,
    projection,
    bag_ids,
    bag_lengths,
    table_width,
):
    hbm = pl.BlockSpec(memory_space=pltpu.HBM)
    vmem = pl.BlockSpec(memory_space=pltpu.VMEM)
    ids = jnp.transpose(bag_ids[0], (1, 2, 0))
    lens = jnp.transpose(bag_lengths[0], (1, 0))
    return pl.pallas_call(
        kernel,
        out_shape=(
            jax.ShapeDtypeStruct((HIDDEN, FEATS), BF16),
            jax.ShapeDtypeStruct((HIDDEN, FEATS), BF16),
            jax.ShapeDtypeStruct((1, 8, PEERS * 1024), BF16),
        ),
        in_specs=[pl.BlockSpec(memory_space=pltpu.SMEM)] + [hbm] * 8,
        out_specs=(vmem, vmem, vmem),
        scratch_shapes=[
            pltpu.VMEM((ROWS, FEATS), BF16),
            pltpu.VMEM((FEATS, ROWS), BF16),
            pltpu.VMEM((HIDDEN, FEATS), BF16),
            pltpu.VMEM((HIDDEN, FEATS), BF16),
            pltpu.VMEM((TABLES, LANES, LANES), F32),
            pltpu.VMEM((TABLES, LANES, LANES), BF16),
            pltpu.VMEM((TABLES, 16, LANES), jnp.int32),
            pltpu.VMEM((TABLES, LANES), jnp.int32),
            pltpu.VMEM((HIDDEN, ROWS), BF16),
            pltpu.VMEM((HIDDEN, ROWS), F32),
            pltpu.VMEM((HIDDEN, ROWS), F32),
            pltpu.VMEM((2 * PIECES, HIDDEN, PIECE), F32),
            pltpu.VMEM((2 * PIECES, HIDDEN, PIECE), BF16),
            pltpu.VMEM((2 * PIECES, 3, SHARE, PIECE), BF16),
            pltpu.VMEM((2 * PIECES, 4, SHARE, PIECE), BF16),
            pltpu.VMEM((2, HIDDEN, FEATS), BF16),
            pltpu.VMEM((PEERS, 16, 512), BF16),
            pltpu.VMEM((PEERS, 16, 512), BF16),
            pltpu.SemaphoreType.DMA((8,)),
            pltpu.SemaphoreType.DMA((COPIES,)),
            pltpu.SemaphoreType.DMA((COPIES,)),
        ],
        compiler_params=pltpu.CompilerParams(
            collective_id=0, has_side_effects=True, vmem_limit_bytes=40 * 2**20
        ),
        cost_estimate=pl.CostEstimate(
            flops=2 * 4 * HIDDEN * ROWS * FEATS, bytes_accessed=8 * 2**20, transcendentals=HIDDEN * ROWS
        ),
    )(
        table_width,
        top_input,
        cotangent,
        w_first,
        w_second,
        sectioned_rows[0],
        projection,
        ids,
        lens,
    )


def solution(mesh):
    placed = (
        P("replica", None),
        P("table", "replica"),
        P("table", None),
        P("table", None),
        P("replica", "table", None, None),
        P("table", None, None),
        P("replica", None, "table", None),
        P("replica", None, "table"),
        P("table"),
    )
    return jax.shard_map(
        shards,
        mesh=mesh,
        in_specs=placed,
        out_specs=(P("table", None), P("table", None), P("replica", "table", None)),
        check_vma=False,
    )
```

time: 260 us -> 89.3 us (0.34)
  the two profiles are of different devices: /device:TPU:122 before, /device:TPU:64 now
where the time goes in v1:
time: 89.3 us; the launch traced here: 88.9 us
  Pallas kernels  76.6 us (86%)
  local copies, waits for them, and re-layouts  11.6 us (13%)
    pallas_call x1, Pallas kernels, shards(): pl.pallas_call(kernel, out_shape=(jax.ShapeDtypeStruct((HIDDEN, FEATS), B...  76.6 us
    unnamed x21, local copies, waits for them, and re-layouts  11.6 us

profile of v1, /device:TPU:64, one launch (start us, length us, event | category | flops | bytes accessed | tf_op | source)
XLA Modules:
  0.0 88.9 jit_solution(5141848219838805154)
XLA Ops:
  0.6 0.0 copy-start
  0.6 2.2 %copy-done = bf16[1024,2048]{1,0:T(8,128)(2,1)S(1)} copy-done((bf16[1024,2048]{1,0:T(8,128)(2,1)S(1)}, bf16[1024,2048]{1,0:T(8,128)(2,1)}, u32[]{:S(2)}) %copy-start) | copy-done | bytes 4194328
  2.8 0.0 copy-start.1
  2.8 1.2 %copy-done.1 = f32[1,4,256,256]{3,2,1,0:T(8,128)S(1)} copy-done((f32[1,4,256,256]{3,2,1,0:T(8,128)S(1)}, f32[1,4,256,256]{3,2,1,0:T(8,128)}, u32[]{:S(2)}) %copy-start.1) | copy-done | bytes 1048600
  4.0 0.0 copy-start.2
  4.0 1.0 %copy-done.2 = bf16[4,256,256]{2,1,0:T(8,128)(2,1)S(1)} copy-done((bf16[4,256,256]{2,1,0:T(8,128)(2,1)S(1)}, bf16[4,256,256]{2,1,0:T(8,128)(2,1)}, u32[]{:S(2)}) %copy-start.2) | copy-done | bytes 524312
  5.1 0.0 copy-start.3
  5.1 0.9 %copy-done.3 = bf16[64,2048]{1,0:T(8,128)(2,1)S(1)} copy-done((bf16[64,2048]{1,0:T(8,128)(2,1)S(1)}, bf16[64,2048]{1,0:T(8,128)(2,1)}, u32[]{:S(2)}) %copy-start.3) | copy-done | bytes 262168
  6.0 0.0 copy-start.4
  6.0 0.9 %copy-done.4 = bf16[64,2048]{1,0:T(8,128)(2,1)S(1)} copy-done((bf16[64,2048]{1,0:T(8,128)(2,1)S(1)}, bf16[64,2048]{1,0:T(8,128)(2,1)}, u32[]{:S(2)}) %copy-start.4) | copy-done | bytes 262168
  7.0 0.0 copy-start.5
  7.0 0.9 %copy-done.5 = bf16[64,1024]{1,0:T(8,128)(2,1)S(1)} copy-done((bf16[64,1024]{1,0:T(8,128)(2,1)S(1)}, bf16[64,1024]{1,0:T(8,128)(2,1)}, u32[]{:S(2)}) %copy-start.5) | copy-done | bytes 131096
  7.9 0.0 copy-start.6
  7.9 0.8 copy-done.6
  8.7 0.0 copy-start.7
  8.7 0.7 copy-done.7
  9.4 0.0 copy-start.8
  9.4 0.7 copy-done.8
  10.1 76.6 %shard_map.112 = (bf16[64,2048]{1,0:T(8,128)(2,1)S(1)}, bf16[64,2048]{1,0:T(8,128)(2,1)S(1)}, bf16[1,8,32768]{2,1,0:T(8,128)(2,1)S(1)}) custom-call(s32[4]{0:T(128)S(1)} %copy-done.8, bf16[1024,2048]{1,0:T(8,128)(2,1)S(1)} %copy-done, bf16[64,1024]{1,0:T(8,128)(2,1)S(1)} %copy-done.5, bf16[64,2048]{1,0:T(8,128)(2,1)S(1)} %copy-done.3, ...), custom_call_target="tpu_custom_call" | custom-call | flops 1073741824 | bytes 8388608 | tf_op jit(solution)/shard_map/pallas_call | solution.py:356
  86.7 0.7 copy.15
  87.4 0.7 copy.16
  88.1 0.8 copy.17
Async XLA Ops:
  0.6 2.2 %copy-start = (bf16[1024,2048]{1,0:T(8,128)(2,1)S(1)}, bf16[1024,2048]{1,0:T(8,128)(2,1)}, u32[]{:S(2)}) copy-start(bf16[1024,2048]{1,0:T(8,128)(2,1)} %top_hbm.1) | copy-start | bytes 12582916
  2.8 1.2 %copy-start.1 = (f32[1,4,256,256]{3,2,1,0:T(8,128)S(1)}, f32[1,4,256,256]{3,2,1,0:T(8,128)}, u32[]{:S(2)}) copy-start(f32[1,4,256,256]{3,2,1,0:T(8,128)} %param.13) | copy-start | bytes 3145732
  4.0 1.0 %copy-start.2 = (bf16[4,256,256]{2,1,0:T(8,128)(2,1)S(1)}, bf16[4,256,256]{2,1,0:T(8,128)(2,1)}, u32[]{:S(2)}) copy-start(bf16[4,256,256]{2,1,0:T(8,128)(2,1)} %proj_hbm.1) | copy-start | bytes 1572868
  5.1 0.9 %copy-start.3 = (bf16[64,2048]{1,0:T(8,128)(2,1)S(1)}, bf16[64,2048]{1,0:T(8,128)(2,1)}, u32[]{:S(2)}) copy-start(bf16[64,2048]{1,0:T(8,128)(2,1)} %first_hbm.1) | copy-start | bytes 786436
  6.0 0.9 %copy-start.4 = (bf16[64,2048]{1,0:T(8,128)(2,1)S(1)}, bf16[64,2048]{1,0:T(8,128)(2,1)}, u32[]{:S(2)}) copy-start(bf16[64,2048]{1,0:T(8,128)(2,1)} %second_hbm.1) | copy-start | bytes 786436
  7.0 0.9 %copy-start.5 = (bf16[64,1024]{1,0:T(8,128)(2,1)S(1)}, bf16[64,1024]{1,0:T(8,128)(2,1)}, u32[]{:S(2)}) copy-start(bf16[64,1024]{1,0:T(8,128)(2,1)} %cot_hbm.1) | copy-start | bytes 393220
  7.9 0.8 copy-start.6
  8.7 0.7 copy-start.7
  9.4 0.7 copy-start.8

commit v2 on v1

--- a/solution.py
+++ b/solution.py
@@ -26,7 +26,7 @@
 CORE_AT = HALF_AT + 8
 PIECE_AT = CORE_AT + 16
 SPREAD_AT = PIECE_AT + 9 * 2 * PIECES
-COPIES = SPREAD_AT + PEERS - 1
+COPIES = SPREAD_AT + 7 + 3
 
 
 def wrap(value, size):
@@ -34,7 +34,7 @@
 
 
 def kernel(
-    widths,
+    widths_hbm,
     top_hbm,
     cot_hbm,
     first_hbm,
@@ -54,6 +54,7 @@
     proj,
     ids,
     lens,
+    widths,
     hidden,
     slope,
     d_hidden,
@@ -63,6 +64,7 @@
     z_in,
     result,
     spread,
+    passing,
     arrived,
     local_sem,
     send_sem,
@@ -112,7 +114,23 @@
         return copy
 
     mine = block(x, z, c)
+    run = z * 2 + c
     load_cot = local(0, cot_hbm, mine)
+
+    barrier = pltpu.get_barrier_semaphore()
+
+    def greet(to_table, to_replica):
+        pl.semaphore_signal(
+            barrier, inc=1, device_id=(to_table, to_replica), device_id_type=MESH
+        )
+
+    for k in range(1, 8):
+        greet(x * 8 + wrap(run + k, 8), replica)
+    for k in range(1, 4):
+        greet(wrap(x + k, 4) * 8 + run, replica)
+    for k in range(1, 4):
+        greet(table, wrap(y + k, 4) * 4 + zh)
+        greet(table, y * 4 + wrap(zh + k, 4))
     load_first = local(1, first_hbm, first)
     load_top = local(2, top_hbm, top)
     load_ids = local(3, ids_hbm, ids)
@@ -120,41 +138,30 @@
     load_rows = local(5, rows_hbm, rows)
     load_proj = local(6, proj_hbm, proj)
     load_second = local(7, second_hbm, second)
-
-    barrier = pltpu.get_barrier_semaphore()
-    for k in range(1, PEERS):
-        pl.semaphore_signal(
-            barrier, inc=1, device_id=(wrap(table + k, PEERS), replica), device_id_type=MESH
-        )
-    for k in range(1, 4):
-        pl.semaphore_signal(
-            barrier, inc=1, device_id=(table, wrap(y + k, 4) * 4 + zh), device_id_type=MESH
-        )
-        pl.semaphore_signal(
-            barrier, inc=1, device_id=(table, y * 4 + wrap(zh + k, 4)), device_id_type=MESH
-        )
+    load_widths = local(8, widths_hbm, widths)
     load_cot.wait()
-    pl.semaphore_wait(barrier, PEERS - 1 + 6)
-
+    pl.semaphore_wait(barrier, 16)
+
+    run_z = (z, z + 1 - 2 * lax.rem(z, 2), wrap(z + 2, 4), 3 - z)
     x_up, x_down, x_far = wrap(x + 1, 4), wrap(x - 1, 4), wrap(x + 2, 4)
     columns = (x, x_up, x_down, x_far)
 
     def to_core(which, j):
-        ref = block(columns[which], wrap(z + j, 4), c)
+        ref = block(columns[which], run_z[j], c)
         send(CORE_AT + which * 4 + j, ref, ref, table_of(x, z, 1 - c), replica)
 
     def from_core(which):
         for j in range(4):
-            ref = block(columns[which], wrap(z + j, 4), 1 - c)
+            ref = block(columns[which], run_z[j], 1 - c)
             receive(CORE_AT + which * 4 + j, ref)
 
     def to_x(j):
-        ref = block(x, wrap(z + j, 4), c)
+        ref = block(x, run_z[j], c)
         send(X_AT + j, ref, ref, table_of(x_up, z, c), replica)
         send(X_AT + 4 + j, ref, ref, table_of(x_down, z, c), replica)
 
     def from_x(j):
-        zj = wrap(z + j, 4)
+        zj = run_z[j]
         receive(X_AT + j, block(x_down, zj, c))
         ref = block(x_down, zj, c, 0)
         send(HALF_AT + j, ref, ref, table_of(x_up, z, c), replica)
@@ -165,14 +172,15 @@
         to_core(1, j)
 
     def from_far(j):
-        zj = wrap(z + j, 4)
+        zj = run_z[j]
         receive(HALF_AT + j, block(x_far, zj, c, 0))
         receive(HALF_AT + 4 + j, block(x_far, zj, c, 1))
         to_core(3, j)
 
-    for k in (1, 3, 2):
-        send(Z_AT + k - 1, mine, mine, table_of(x, wrap(z + k, 4), c), replica)
+    send(Z_AT, mine, mine, table_of(x, run_z[1], c), replica)
     to_x(0)
+    for v in (3, 2):
+        send(Z_AT + v - 1, mine, mine, table_of(x, run_z[v], c), replica)
     to_core(0, 0)
 
     load_first.wait()
@@ -194,6 +202,7 @@
     load_lens.wait()
     load_rows.wait()
     load_proj.wait()
+    load_widths.wait()
 
     def pool(t):
         slots = lax.broadcasted_iota(jnp.int32, (16, LANES), 0)
@@ -218,7 +227,9 @@
     def pool_pair(t):
         upper = pool(t).reshape(PEERS, 8, LANES)
         lower = pool(t + 2).reshape(PEERS, 8, LANES)
-        spread[:, :, t * LANES : (t + 1) * LANES] = jnp.concatenate([upper, lower], 1).astype(BF16)
+        both = jnp.concatenate([upper, lower], 1).astype(BF16)
+        for to in range(4):
+            spread[:, to, :, t * LANES : (t + 1) * LANES] = both[to * 8 : (to + 1) * 8]
 
     def column_step(which):
         at = pl.ds(pl.multiple_of(columns[which] * PIECE, PIECE), PIECE)
@@ -282,28 +293,52 @@
         for k in range(1, 4):
             receive(PIECE_AT + 9 * p + 6 + k - 1, result.at[which, share(wrap(y - k, 4)), at])
 
+    def spread_run():
+        for k in range(1, 8):
+            to = wrap(run + k, 8)
+            send(SPREAD_AT + k - 1, spread.at[to], passing.at[:, run], x * 8 + to, replica)
+        passing[:, run] = spread[run]
+
+    def spread_x():
+        for k in range(1, 8):
+            receive(SPREAD_AT + k - 1, passing.at[:, wrap(run - k, 8)])
+        for k in (1, 3, 2):
+            to = wrap(x + k, 4)
+            send(SPREAD_AT + 7 + k - 1, passing.at[to], arrived.at[x], to * 8 + run, replica)
+        arrived[x] = passing[x]
+
+    def place_pooled():
+        for k in (1, 3, 2):
+            receive(SPREAD_AT + 7 + k - 1, arrived.at[wrap(x - k, 4)])
+
+        def place(j, carry):
+            value = arrived[lax.div(j, 8), lax.rem(j, 8)].astype(F32)
+            start = pl.multiple_of(j * 1024, 1024)
+            out_pooled[0, :, pl.ds(start, 512)] = value[:8].astype(BF16)
+            out_pooled[0, :, pl.ds(start + 512, 512)] = value[8:].astype(BF16)
+            return carry
+
+        lax.fori_loop(0, PEERS, place, 0)
+
+    pool_pair(0)
+    pool_pair(1)
     from_x(0)
-    pool_pair(0)
-    for k in (1, 3, 2):
-        receive(Z_AT + k - 1, block(x, wrap(z - k, 4), c))
-        to_x(4 - k)
-        to_core(0, 4 - k)
-    pool_pair(1)
+    for v in (1, 3, 2):
+        receive(Z_AT + v - 1, block(x, run_z[v], c))
+        to_x(v)
+        to_core(0, v)
+    spread_run()
     load_second.wait()
     from_core(0)
     column_step(0)
-    for j in (3, 1, 2):
+    for j in (1, 3, 2):
         from_x(j)
-    for k in range(1, PEERS):
-        to = wrap(table + k, PEERS)
-        send(SPREAD_AT + k - 1, spread.at[to], arrived.at[table], to, replica)
-    arrived[table] = spread[table]
     exchange(0)
     from_core(1)
     column_step(1)
     from_core(2)
     column_step(2)
-    for j in (0, 3, 1, 2):
+    for j in (0, 1, 3, 2):
         from_far(j)
     exchange(1)
     exchange(2)
@@ -315,21 +350,18 @@
             PIECES + q,
             jnp.dot(d_pre, top[:, q * PIECE : (q + 1) * PIECE], preferred_element_type=F32),
         )
+    spread_x()
     for p in range(3, 2 * PIECES):
         exchange(p)
-    for p in range(2 * PIECES):
+    finish(0)
+    finish(1)
+    finish(2)
+    place_pooled()
+    for copy in sent:
+        copy.wait_send()
+    sent.clear()
+    for p in range(3, 2 * PIECES):
         finish(p)
-    for k in range(1, PEERS):
-        receive(SPREAD_AT + k - 1, arrived.at[wrap(table - k, PEERS)])
-
-    def place(j, carry):
-        value = arrived[j].astype(F32)
-        start = pl.multiple_of(j * 1024, 1024)
-        out_pooled[0, :, pl.ds(start, 512)] = value[:8].astype(BF16)
-        out_pooled[0, :, pl.ds(start + 512, 512)] = value[8:].astype(BF16)
-        return carry
-
-    lax.fori_loop(0, PEERS, place, 0)
     for p in range(2 * PIECES):
         collect(p)
     out_first[...] = result[0]
@@ -360,7 +392,7 @@
             jax.ShapeDtypeStruct((HIDDEN, FEATS), BF16),
             jax.ShapeDtypeStruct((1, 8, PEERS * 1024), BF16),
         ),
-        in_specs=[pl.BlockSpec(memory_space=pltpu.SMEM)] + [hbm] * 8,
+        in_specs=[hbm] * 9,
         out_specs=(vmem, vmem, vmem),
         scratch_shapes=[
             pltpu.VMEM((ROWS, FEATS), BF16),
@@ -371,6 +403,7 @@
             pltpu.VMEM((TABLES, LANES, LANES), BF16),
             pltpu.VMEM((TABLES, 16, LANES), jnp.int32),
             pltpu.VMEM((TABLES, LANES), jnp.int32),
+            pltpu.SMEM((TABLES,), jnp.int32),
             pltpu.VMEM((HIDDEN, ROWS), BF16),
             pltpu.VMEM((HIDDEN, ROWS), F32),
             pltpu.VMEM((HIDDEN, ROWS), F32),
@@ -379,9 +412,10 @@
             pltpu.VMEM((2 * PIECES, 3, SHARE, PIECE), BF16),
             pltpu.VMEM((2 * PIECES, 4, SHARE, PIECE), BF16),
             pltpu.VMEM((2, HIDDEN, FEATS), BF16),
-            pltpu.VMEM((PEERS, 16, 512), BF16),
-            pltpu.VMEM((PEERS, 16, 512), BF16),
-            pltpu.SemaphoreType.DMA((8,)),
+            pltpu.VMEM((8, 4, 16, 512), BF16),
+            pltpu.VMEM((4, 8, 16, 512), BF16),
+            pltpu.VMEM((4, 8, 16, 512), BF16),
+            pltpu.SemaphoreType.DMA((9,)),
             pltpu.SemaphoreType.DMA((COPIES,)),
             pltpu.SemaphoreType.DMA((COPIES,)),
         ],
@@ -392,15 +426,20 @@
             flops=2 * 4 * HIDDEN * ROWS * FEATS, bytes_accessed=8 * 2**20, transcendentals=HIDDEN * ROWS
         ),
     )(
-        table_width,
-        top_input,
-        cotangent,
-        w_first,
-        w_second,
-        sectioned_rows[0],
-        projection,
-        ids,
-        lens,
+        *(
+            pltpu.with_memory_space_constraint(value, pltpu.HBM)
+            for value in (
+                table_width,
+                top_input,
+                cotangent,
+                w_first,
+                w_second,
+                sectioned_rows[0],
+                projection,
+                ids,
+                lens,
+            )
+        )
     )
 
 

time: 89.3 us -> 72.9 us (0.82)
  the two profiles are of different devices: /device:TPU:64 before, /device:TPU:68 now
where the time goes in v2:
time: 72.9 us; the launch traced here: 72.8 us
  Pallas kernels  70 us (96%)
  local copies, waits for them, and re-layouts  2.2 us (3%)
    pallas_call x1, Pallas kernels, shards(): pl.pallas_call(kernel, out_shape=(jax.ShapeDtypeStruct((HIDDEN, FEATS), B...  70 us
    unnamed x3, local copies, waits for them, and re-layouts  2.2 us

profile of v2, /device:TPU:68, one launch (start us, length us, event | category | flops | bytes accessed | tf_op | source)
XLA Modules:
  0.0 72.8 jit_solution(4077807905875200358)
XLA Ops:
  0.6 70.0 %shard_map.112 = (bf16[64,2048]{1,0:T(8,128)(2,1)S(1)}, bf16[64,2048]{1,0:T(8,128)(2,1)S(1)}, bf16[1,8,32768]{2,1,0:T(8,128)(2,1)S(1)}) custom-call(s32[4]{0:T(128)} %widths_hbm.1, bf16[1024,2048]{1,0:T(8,128)(2,1)} %top_hbm.1, bf16[64,1024]{1,0:T(8,128)(2,1)} %cot_hbm.1, bf16[64,2048]{1,0:T(8,128)(2,1)} %first_hbm.1, bf16[64,2048]{1,0:T(8,128)(2,1)} %second_hbm.1, ...), custom_call_target="tpu_custom_call" | custom-call | flops 1073741824 | bytes 8388608 | tf_op jit(solution)/shard_map/pallas_call | solution.py:388
  70.6 0.7 copy.15
  71.3 0.7 copy.16
  72.0 0.8 %copy.17 = bf16[1,8,32768]{2,1,0:T(8,128)(2,1)} copy(bf16[1,8,32768]{2,1,0:T(8,128)(2,1)S(1)} %get-tuple-element.8) | data formatting | bytes 1048576

commit v3 on v2

v3 whole, which is shorter than its diff:
```python
import jax
import jax.numpy as jnp
from jax import lax
from jax.experimental import pallas as pl
from jax.experimental.pallas import tpu as pltpu
from jax.sharding import PartitionSpec as P

MESH = pl.DeviceIdType.MESH
F32 = jnp.float32
BF16 = jnp.bfloat16

HIDDEN = 64
ROWS = 1024
FEATS = 2048
BLOCK = 64
RUN = 512
LINE = 256
CHUNKS = 4
CHUNK = ROWS // CHUNKS
PIECES = 4
PIECE = FEATS // PIECES
SHARE = 16
PEERS = 32
TABLES = 4
LANES = 256

Z_AT = 0
CORE_AT = Z_AT + 3 * CHUNKS
PARTIAL_AT = CORE_AT + 1 + 3 * CHUNKS
WEIGHT_AT = PARTIAL_AT + 3 * CHUNKS
HIDDEN_AT = WEIGHT_AT + 3
FIRST_AT = HIDDEN_AT + 3
SECOND_AT = FIRST_AT + 8 * PIECES
SPREAD_AT = SECOND_AT + 13
COPIES = SPREAD_AT + 7 + 3


def wrap(value, size):
    return lax.rem(value + size, size)


def kernel(
    widths_hbm,
    top_hbm,
    cot_hbm,
    first_hbm,
    second_hbm,
    rows_hbm,
    proj_hbm,
    ids_hbm,
    lens_hbm,
    out_first,
    out_second,
    out_pooled,
    top,
    cot,
    first,
    second,
    rows,
    proj,
    ids,
    lens,
    widths,
    hidden,
    slope,
    d_hidden,
    d_hidden_b,
    d_in,
    part,
    y_in,
    z_in,
    result,
    part2_b,
    y_own2,
    y_in2,
    z_in2,
    final2,
    result2,
    spread,
    passing,
    arrived,
    local_sem,
    send_sem,
    recv_sem,
):
    table = lax.axis_index("table")
    replica = lax.axis_index("replica")
    x = lax.div(table, 8)
    z = lax.rem(lax.div(table, 2), 4)
    c = lax.rem(table, 2)
    y = lax.div(replica, 4)
    zh = lax.rem(replica, 4)

    run = z * 2 + c

    def block(z_, c_, chunk=None):
        at = pl.ds(pl.multiple_of((z_ * 2 + c_) * BLOCK, BLOCK), BLOCK)
        if chunk is None:
            return cot.at[at]
        return cot.at[at, pl.ds(chunk * CHUNK, CHUNK)]

    def unit(x_):
        return pl.ds(pl.multiple_of(x_ * HIDDEN, HIDDEN), HIDDEN)

    def remote(number, src, dst, to_table, to_replica):
        return pltpu.make_async_remote_copy(
            src_ref=src,
            dst_ref=dst,
            send_sem=send_sem.at[number],
            recv_sem=recv_sem.at[number],
            device_id=(to_table, to_replica),
            device_id_type=MESH,
        )

    sent = []

    def send(number, src, dst, to_table, to_replica):
        copy = remote(number, src, dst, to_table, to_replica)
        copy.start()
        sent.append(copy)

    def receive(number, dst):
        remote(number, dst, dst, table, replica).wait_recv()

    def local(number, src, dst):
        copy = pltpu.make_async_copy(src, dst, local_sem.at[number])
        copy.start()
        return copy

    mine = block(z, c)
    load_cot = local(0, cot_hbm, mine)

    barrier = pltpu.get_barrier_semaphore()

    def greet(to_table, to_replica):
        pl.semaphore_signal(
            barrier, inc=1, device_id=(to_table, to_replica), device_id_type=MESH
        )

    for k in range(1, 8):
        greet(x * 8 + wrap(run + k, 8), replica)
    for k in range(1, 4):
        greet(wrap(x + k, 4) * 8 + run, replica)
    for k in range(1, 4):
        greet(table, wrap(y + k, 4) * 4 + zh)
    pairs = (y * 4 + zh + 1 - 2 * lax.rem(zh, 2), y * 4 + 3 - zh)
    greet(table, pairs[0])
    greet(table, pairs[1])
    load_first = local(1, first_hbm, first)
    load_top = local(2, top_hbm, top)
    load_ids = local(3, ids_hbm, ids)
    load_lens = local(4, lens_hbm, lens)
    load_rows = local(5, rows_hbm, rows)
    load_proj = local(6, proj_hbm, proj)
    run_at = pl.ds(pl.multiple_of(x * RUN, RUN), RUN)
    load_second = local(7, second_hbm.at[:, run_at], second.at[unit(x)])
    load_widths = local(8, widths_hbm, widths)
    load_cot.wait()
    pl.semaphore_wait(barrier, 15)

    run_z = (z, z + 1 - 2 * lax.rem(z, 2), wrap(z + 2, 4), 3 - z)
    def to_x(number, src, dst, k):
        send(number + k - 1, src, dst, wrap(x + k, 4) * 8 + run, replica)

    for r in range(CHUNKS):
        for v in (1, 3, 2):
            ref = block(z, c, r)
            send(Z_AT + 3 * r + v - 1, ref, ref, x * 8 + run_z[v] * 2 + c, replica)
    partner = x * 8 + z * 2 + 1 - c
    send(CORE_AT, mine, mine, partner, replica)

    for k in (1, 3, 2):
        to = pl.ds(pl.multiple_of(wrap(x + k, 4) * RUN, RUN), RUN)
        to_x(WEIGHT_AT, second_hbm.at[:, to], second.at[unit(x)], k)

    load_first.wait()
    load_top.wait()

    def forward(step, carry):
        at = pl.ds(pl.multiple_of(step * 256, 256), 256)
        pre = lax.dot_general(
            first[...], top[at, :], (((1,), (1,)), ((), ())), preferred_element_type=F32
        )
        s = 1.0 / (1.0 + jnp.exp(-pre))
        hidden[unit(x), at] = (pre * s).astype(BF16)
        slope[:, at] = s * (1.0 + pre * (1.0 - s))
        return carry

    lax.fori_loop(0, 4, forward, 0)
    for k in (1, 3, 2):
        to_x(HIDDEN_AT, hidden.at[unit(x)], hidden.at[unit(x)], k)

    load_ids.wait()
    load_lens.wait()
    load_rows.wait()
    load_proj.wait()
    load_widths.wait()

    def pool(t):
        slots = lax.broadcasted_iota(jnp.int32, (16, LANES), 0)
        live = jnp.where(slots < lens[t : t + 1, :], ids[t], -1)
        numbers = lax.broadcasted_iota(jnp.int32, (LANES, LANES), 0)
        counts = jnp.zeros((LANES, LANES), F32)
        for k in range(16):
            counts = counts + jnp.where(live[k : k + 1, :] == numbers, 1.0, 0.0)
        counts = counts.T.astype(BF16)
        whole = rows[t]
        high = whole.astype(BF16)
        rest = whole - high.astype(F32)
        middle = rest.astype(BF16)
        low = (rest - middle.astype(F32)).astype(BF16)
        pooled = jnp.dot(counts, low, preferred_element_type=F32)
        pooled = pooled + jnp.dot(counts, middle, preferred_element_type=F32)
        pooled = pooled + jnp.dot(counts, high, preferred_element_type=F32)
        lanes = lax.broadcasted_iota(jnp.int32, (LANES, LANES), 1)
        kept = jnp.where(lanes < widths[t], pooled, 0.0).astype(BF16)
        return jnp.dot(kept, proj[t], preferred_element_type=F32)

    def pool_pair(t):
        upper = pool(t).reshape(PEERS, 8, LANES)
        lower = pool(t + 2).reshape(PEERS, 8, LANES)
        both = jnp.concatenate([upper, lower], 1).astype(BF16)
        for to in range(4):
            spread[:, to, :, t * LANES : (t + 1) * LANES] = both[to * 8 : (to + 1) * 8]

    def share(y_):
        return pl.ds(pl.multiple_of(y_ * SHARE, SHARE), SHARE)

    def gather(r):
        for v in (1, 3, 2):
            ref = block(run_z[v], c, r)
            receive(Z_AT + 3 * r + v - 1, ref)
            send(CORE_AT + 1 + 3 * r + v - 1, ref, ref, partner, replica)

    def products(r):
        if r == 0:
            load_second.wait()
            for k in range(1, 4):
                receive(WEIGHT_AT + k - 1, second.at[unit(wrap(x - k, 4))])
            receive(CORE_AT, block(z, 1 - c))
        for v in (1, 3, 2):
            receive(CORE_AT + 1 + 3 * r + v - 1, block(run_z[v], 1 - c, r))
        at = slice(r * CHUNK, (r + 1) * CHUNK)
        value = jnp.dot(second[...], cot[:, at], preferred_element_type=F32)
        d_hidden[:, at] = value
        d_hidden_b[:, at] = value.astype(BF16)
        at = pl.ds(r * CHUNK, CHUNK)
        for k in (2, 1, 3):
            to_x(
                PARTIAL_AT + 3 * r,
                d_hidden_b.at[unit(wrap(x + k, 4)), at],
                d_in.at[k - 1, :, at],
                k,
            )

    def d_pre(r):
        at = pl.ds(r * CHUNK, CHUNK)
        total = d_hidden[unit(x), at]
        for k in (1, 3, 2):
            receive(PARTIAL_AT + 3 * r + k - 1, d_in.at[k - 1, :, at])
        for k in range(1, 4):
            total = total + d_in[k - 1, :, at].astype(F32)
        return (total * slope[:, at]).astype(BF16)

    def first_chunk(r):
        value = jnp.dot(d_pre(r), top[r * CHUNK : (r + 1) * CHUNK], preferred_element_type=F32)
        if r == 0:
            part[...] = value
        else:
            part[...] += value

    def first_last():
        r = CHUNKS - 1
        left = d_pre(r)
        for p in range(PIECES):
            at = slice(p * PIECE, (p + 1) * PIECE)
            value = part[:, at] + jnp.dot(
                left, top[r * CHUNK :, at], preferred_element_type=F32
            )
            part[:, at] = value
            at = pl.ds(p * PIECE, PIECE)
            for k in (2, 1, 3):
                to = wrap(y + k, 4)
                send(
                    FIRST_AT + 8 * p + k - 1,
                    part.at[share(to), at],
                    y_in.at[k - 1, :, at],
                    table,
                    to * 4 + zh,
                )

    def exchange(p):
        at = pl.ds(p * PIECE, PIECE)
        total = part[share(y), at]
        for k in (1, 3, 2):
            receive(FIRST_AT + 8 * p + k - 1, y_in.at[k - 1, :, at])
        for k in range(1, 4):
            total = total + y_in[k - 1, :, at]
        z_in[p, 0] = total.astype(BF16)
        send(FIRST_AT + 8 * p + 3, z_in.at[p, 0], z_in.at[p, 1], table, pairs[p % 2])

    def pair(p):
        receive(FIRST_AT + 8 * p + 3, z_in.at[p, 1])
        z_in[p, 2] = (z_in[p, 0].astype(F32) + z_in[p, 1].astype(F32)).astype(BF16)
        send(FIRST_AT + 8 * p + 4, z_in.at[p, 2], z_in.at[p, 3], table, pairs[1 - p % 2])

    def finish(p):
        receive(FIRST_AT + 8 * p + 4, z_in.at[p, 3])
        at = pl.ds(p * PIECE, PIECE)
        result[share(y), at] = (z_in[p, 2].astype(F32) + z_in[p, 3].astype(F32)).astype(BF16)
        ref = result.at[share(y), at]
        for k in (2, 1, 3):
            send(FIRST_AT + 8 * p + 5 + k - 1, ref, ref, table, wrap(y + k, 4) * 4 + zh)

    def collect(p):
        for k in (1, 3, 2):
            ref = result.at[share(wrap(y - k, 4)), pl.ds(p * PIECE, PIECE)]
            receive(FIRST_AT + 8 * p + 5 + k - 1, ref)

    def second_out():
        for k in range(1, 4):
            receive(HIDDEN_AT + k - 1, hidden.at[unit(wrap(x - k, 4))])
        value = lax.dot_general(
            hidden[...], cot[...], (((1,), (1,)), ((), ())), preferred_element_type=F32
        )
        y_own2[...] = value
        part2_b[...] = value.astype(BF16)
        for k in (2, 1, 3):
            to = wrap(y + k, 4)
            send(SECOND_AT + k - 1, part2_b.at[unit(to)], y_in2.at[k - 1], table, to * 4 + zh)

    def second_exchange():
        for k in (1, 3, 2):
            receive(SECOND_AT + k - 1, y_in2.at[k - 1])
        total = y_own2[unit(y), :]
        for k in range(1, 4):
            total = total + y_in2[k - 1].astype(F32)
        for h in range(2):
            z_in2[h, 0] = total[:, h * 256 : (h + 1) * 256].astype(BF16)
            send(SECOND_AT + 3 + h, z_in2.at[h, 0], z_in2.at[h, 1], table, pairs[h])

    def second_pair():
        for h in range(2):
            receive(SECOND_AT + 3 + h, z_in2.at[h, 1])
            z_in2[h, 2] = (z_in2[h, 0].astype(F32) + z_in2[h, 1].astype(F32)).astype(BF16)
            send(SECOND_AT + 5 + h, z_in2.at[h, 2], z_in2.at[h, 3], table, pairs[1 - h])

    def second_finish():
        for h in range(2):
            receive(SECOND_AT + 5 + h, z_in2.at[h, 3])
            final2[unit(y), h * 256 : (h + 1) * 256] = (
                z_in2[h, 2].astype(F32) + z_in2[h, 3].astype(F32)
            ).astype(BF16)
        ref = final2.at[unit(y)]
        for k in (2, 1, 3):
            send(SECOND_AT + 7 + k - 1, ref, ref, table, wrap(y + k, 4) * 4 + zh)

    def second_turn():
        for k in (1, 3, 2):
            receive(SECOND_AT + 7 + k - 1, final2.at[unit(wrap(y - k, 4))])
        for k in (2, 1, 3):
            to_x(SECOND_AT + 10, final2.at[unit(wrap(x + k, 4))], result2.at[:, run_at], k)
        result2[:, run_at] = final2[unit(x), :]

    def second_collect():
        for k in (1, 3, 2):
            at = pl.ds(pl.multiple_of(wrap(x - k, 4) * RUN, RUN), RUN)
            receive(SECOND_AT + 10 + k - 1, result2.at[:, at])

    def spread_run():
        for k in range(1, 8):
            to = wrap(run + k, 8)
            send(SPREAD_AT + k - 1, spread.at[to], passing.at[:, run], x * 8 + to, replica)
        passing[:, run] = spread[run]

    def spread_x():
        for k in range(1, 8):
            receive(SPREAD_AT + k - 1, passing.at[:, wrap(run - k, 8)])
        for k in (1, 3, 2):
            to = wrap(x + k, 4)
            send(SPREAD_AT + 7 + k - 1, passing.at[to], arrived.at[x], to * 8 + run, replica)
        arrived[x] = passing[x]

    def place_pooled():
        for k in (1, 3, 2):
            receive(SPREAD_AT + 7 + k - 1, arrived.at[wrap(x - k, 4)])

        def place(j, carry):
            value = arrived[lax.div(j, 8), lax.rem(j, 8)].astype(F32)
            start = pl.multiple_of(j * 1024, 1024)
            out_pooled[0, :, pl.ds(start, 512)] = value[:8].astype(BF16)
            out_pooled[0, :, pl.ds(start + 512, 512)] = value[8:].astype(BF16)
            return carry

        lax.fori_loop(0, PEERS, place, 0)

    pool_pair(0)
    gather(0)
    pool_pair(1)
    gather(1)
    products(0)
    gather(2)
    products(1)
    first_chunk(0)
    gather(3)
    spread_run()
    products(2)
    first_chunk(1)
    products(3)
    second_out()
    first_chunk(2)
    first_last()
    second_exchange()
    spread_x()
    for p in range(PIECES):
        exchange(p)
    second_pair()
    for p in range(PIECES):
        pair(p)
    second_finish()
    for copy in sent:
        copy.wait_send()
    sent.clear()
    place_pooled()
    for p in range(PIECES):
        finish(p)
    second_turn()
    for p in range(PIECES):
        collect(p)
    second_collect()
    out_first[...] = result[...]
    out_second[...] = result2[...]
    for copy in sent:
        copy.wait_send()


def shards(
    top_input,
    cotangent,
    w_first,
    w_second,
    sectioned_rows,
    projection,
    bag_ids,
    bag_lengths,
    table_width,
):
    hbm = pl.BlockSpec(memory_space=pltpu.HBM)
    vmem = pl.BlockSpec(memory_space=pltpu.VMEM)
    ids = jnp.transpose(bag_ids[0], (1, 2, 0))
    lens = jnp.transpose(bag_lengths[0], (1, 0))
    return pl.pallas_call(
        kernel,
        out_shape=(
            jax.ShapeDtypeStruct((HIDDEN, FEATS), BF16),
            jax.ShapeDtypeStruct((HIDDEN, FEATS), BF16),
            jax.ShapeDtypeStruct((1, 8, PEERS * 1024), BF16),
        ),
        in_specs=[hbm] * 9,
        out_specs=(vmem, vmem, vmem),
        scratch_shapes=[
            pltpu.VMEM((ROWS, FEATS), BF16),
            pltpu.VMEM((RUN, ROWS), BF16),
            pltpu.VMEM((HIDDEN, FEATS), BF16),
            pltpu.VMEM((LINE, RUN), BF16),
            pltpu.VMEM((TABLES, LANES, LANES), F32),
            pltpu.VMEM((TABLES, LANES, LANES), BF16),
            pltpu.VMEM((TABLES, 16, LANES), jnp.int32),
            pltpu.VMEM((TABLES, LANES), jnp.int32),
            pltpu.SMEM((TABLES,), jnp.int32),
            pltpu.VMEM((LINE, ROWS), BF16),
            pltpu.VMEM((HIDDEN, ROWS), F32),
            pltpu.VMEM((LINE, ROWS), F32),
            pltpu.VMEM((LINE, ROWS), BF16),
            pltpu.VMEM((3, HIDDEN, ROWS), BF16),
            pltpu.VMEM((HIDDEN, FEATS), F32),
            pltpu.VMEM((3, SHARE, FEATS), F32),
            pltpu.VMEM((PIECES, 4, SHARE, PIECE), BF16),
            pltpu.VMEM((HIDDEN, FEATS), BF16),
            pltpu.VMEM((LINE, RUN), BF16),
            pltpu.VMEM((LINE, RUN), F32),
            pltpu.VMEM((3, HIDDEN, RUN), BF16),
            pltpu.VMEM((2, 4, HIDDEN, RUN // 2), BF16),
            pltpu.VMEM((LINE, RUN), BF16),
            pltpu.VMEM((HIDDEN, FEATS), BF16),
            pltpu.VMEM((8, 4, 16, 512), BF16),
            pltpu.VMEM((4, 8, 16, 512), BF16),
            pltpu.VMEM((4, 8, 16, 512), BF16),
            pltpu.SemaphoreType.DMA((9,)),
            pltpu.SemaphoreType.DMA((COPIES,)),
            pltpu.SemaphoreType.DMA((COPIES,)),
        ],
        compiler_params=pltpu.CompilerParams(
            collective_id=0, has_side_effects=True, vmem_limit_bytes=40 * 2**20
        ),
        cost_estimate=pl.CostEstimate(
            flops=2 * 4 * HIDDEN * ROWS * FEATS, bytes_accessed=8 * 2**20, transcendentals=HIDDEN * ROWS
        ),
    )(
        *(
            pltpu.with_memory_space_constraint(value, pltpu.HBM)
            for value in (
                table_width,
                top_input,
                cotangent,
                w_first,
                w_second,
                sectioned_rows[0],
                projection,
                ids,
                lens,
            )
        )
    )


def solution(mesh):
    placed = (
        P("replica", None),
        P("table", "replica"),
        P("table", None),
        P("table", None),
        P("replica", "table", None, None),
        P("table", None, None),
        P("replica", None, "table", None),
        P("replica", None, "table"),
        P("table"),
    )
    return jax.shard_map(
        shards,
        mesh=mesh,
        in_specs=placed,
        out_specs=(P("table", None), P("table", None), P("replica", "table", None)),
        check_vma=False,
    )
```

time: 72.9 us -> 65 us (0.89)
  the two profiles are of different devices: /device:TPU:68 before, /device:TPU:8 now
where the time goes in v3:
time: 65 us; the launch traced here: 64.9 us
  Pallas kernels  62 us (95%)
  local copies, waits for them, and re-layouts  2.2 us (3%)
    pallas_call x1, Pallas kernels, shards(): pl.pallas_call(kernel, out_shape=(jax.ShapeDtypeStruct((HIDDEN, FEATS), B...  62 us
    unnamed x3, local copies, waits for them, and re-layouts  2.2 us

profile of v3, /device:TPU:8, one launch (start us, length us, event | category | flops | bytes accessed | tf_op | source)
XLA Modules:
  0.0 64.9 jit_solution(13504392979421729738)
XLA Ops:
  0.6 62.0 %shard_map.112 = (bf16[64,2048]{1,0:T(8,128)(2,1)S(1)}, bf16[64,2048]{1,0:T(8,128)(2,1)S(1)}, bf16[1,8,32768]{2,1,0:T(8,128)(2,1)S(1)}) custom-call(s32[4]{0:T(128)} %widths_hbm.1, bf16[1024,2048]{1,0:T(8,128)(2,1)} %top_hbm.1, bf16[64,1024]{1,0:T(8,128)(2,1)} %cot_hbm.1, bf16[64,2048]{1,0:T(8,128)(2,1)} %first_hbm.1, bf16[64,2048]{1,0:T(8,128)(2,1)} %second_hbm.1, ...), custom_call_target="tpu_custom_call" | custom-call | flops 1073741824 | bytes 8388608 | tf_op jit(solution)/shard_map/pallas_call | solution.py:452
  62.7 0.7 %copy.15 = bf16[64,2048]{1,0:T(8,128)(2,1)} copy(bf16[64,2048]{1,0:T(8,128)(2,1)S(1)} %get-tuple-element.6) | data formatting | bytes 524288
  63.4 0.7 %copy.16 = bf16[64,2048]{1,0:T(8,128)(2,1)} copy(bf16[64,2048]{1,0:T(8,128)(2,1)S(1)} %get-tuple-element.7) | data formatting | bytes 524288
  64.1 0.8 %copy.17 = bf16[1,8,32768]{2,1,0:T(8,128)(2,1)} copy(bf16[1,8,32768]{2,1,0:T(8,128)(2,1)S(1)} %get-tuple-element.8) | data formatting | bytes 1048576

commit v4 on v3

--- a/solution.py
+++ b/solution.py
@@ -14,10 +14,11 @@
 FEATS = 2048
 BLOCK = 64
 RUN = 512
+HALF = RUN // 2
 LINE = 256
 CHUNKS = 4
 CHUNK = ROWS // CHUNKS
-PIECES = 4
+PIECES = 2
 PIECE = FEATS // PIECES
 SHARE = 16
 PEERS = 32
@@ -31,7 +32,7 @@
 HIDDEN_AT = WEIGHT_AT + 3
 FIRST_AT = HIDDEN_AT + 3
 SECOND_AT = FIRST_AT + 8 * PIECES
-SPREAD_AT = SECOND_AT + 13
+SPREAD_AT = SECOND_AT + 11 * 2
 COPIES = SPREAD_AT + 7 + 3
 
 
@@ -67,6 +68,7 @@
     d_hidden_b,
     d_in,
     part,
+    part_b,
     y_in,
     z_in,
     result,
@@ -146,6 +148,7 @@
     pairs = (y * 4 + zh + 1 - 2 * lax.rem(zh, 2), y * 4 + 3 - zh)
     greet(table, pairs[0])
     greet(table, pairs[1])
+
     load_first = local(1, first_hbm, first)
     load_top = local(2, top_hbm, top)
     load_ids = local(3, ids_hbm, ids)
@@ -278,12 +281,13 @@
                 left, top[r * CHUNK :, at], preferred_element_type=F32
             )
             part[:, at] = value
+            part_b[:, at] = value.astype(BF16)
             at = pl.ds(p * PIECE, PIECE)
             for k in (2, 1, 3):
                 to = wrap(y + k, 4)
                 send(
                     FIRST_AT + 8 * p + k - 1,
-                    part.at[share(to), at],
+                    part_b.at[share(to), at],
                     y_in.at[k - 1, :, at],
                     table,
                     to * 4 + zh,
@@ -295,7 +299,7 @@
         for k in (1, 3, 2):
             receive(FIRST_AT + 8 * p + k - 1, y_in.at[k - 1, :, at])
         for k in range(1, 4):
-            total = total + y_in[k - 1, :, at]
+            total = total + y_in[k - 1, :, at].astype(F32)
         z_in[p, 0] = total.astype(BF16)
         send(FIRST_AT + 8 * p + 3, z_in.at[p, 0], z_in.at[p, 1], table, pairs[p % 2])
 
@@ -325,47 +329,60 @@
         )
         y_own2[...] = value
         part2_b[...] = value.astype(BF16)
+        for h in range(2):
+            at = pl.ds(h * HALF, HALF)
+            for k in (2, 1, 3):
+                to = wrap(y + k, 4)
+                send(
+                    SECOND_AT + 11 * h + k - 1,
+                    part2_b.at[unit(to), at],
+                    y_in2.at[k - 1, :, at],
+                    table,
+                    to * 4 + zh,
+                )
+
+    def second_exchange(h):
+        at = pl.ds(h * HALF, HALF)
+        total = y_own2[unit(y), at]
+        for k in (1, 3, 2):
+            receive(SECOND_AT + 11 * h + k - 1, y_in2.at[k - 1, :, at])
+        for k in range(1, 4):
+            total = total + y_in2[k - 1, :, at].astype(F32)
+        z_in2[h, 0] = total.astype(BF16)
+        send(SECOND_AT + 11 * h + 3, z_in2.at[h, 0], z_in2.at[h, 1], table, pairs[h])
+
+    def second_pair(h):
+        receive(SECOND_AT + 11 * h + 3, z_in2.at[h, 1])
+        z_in2[h, 2] = (z_in2[h, 0].astype(F32) + z_in2[h, 1].astype(F32)).astype(BF16)
+        send(SECOND_AT + 11 * h + 4, z_in2.at[h, 2], z_in2.at[h, 3], table, pairs[1 - h])
+
+    def second_finish(h):
+        receive(SECOND_AT + 11 * h + 4, z_in2.at[h, 3])
+        at = pl.ds(h * HALF, HALF)
+        final2[unit(y), at] = (z_in2[h, 2].astype(F32) + z_in2[h, 3].astype(F32)).astype(BF16)
+        ref = final2.at[unit(y), at]
         for k in (2, 1, 3):
-            to = wrap(y + k, 4)
-            send(SECOND_AT + k - 1, part2_b.at[unit(to)], y_in2.at[k - 1], table, to * 4 + zh)
-
-    def second_exchange():
-        for k in (1, 3, 2):
-            receive(SECOND_AT + k - 1, y_in2.at[k - 1])
-        total = y_own2[unit(y), :]
-        for k in range(1, 4):
-            total = total + y_in2[k - 1].astype(F32)
-        for h in range(2):
-            z_in2[h, 0] = total[:, h * 256 : (h + 1) * 256].astype(BF16)
-            send(SECOND_AT + 3 + h, z_in2.at[h, 0], z_in2.at[h, 1], table, pairs[h])
-
-    def second_pair():
-        for h in range(2):
-            receive(SECOND_AT + 3 + h, z_in2.at[h, 1])
-            z_in2[h, 2] = (z_in2[h, 0].astype(F32) + z_in2[h, 1].astype(F32)).astype(BF16)
-            send(SECOND_AT + 5 + h, z_in2.at[h, 2], z_in2.at[h, 3], table, pairs[1 - h])
-
-    def second_finish():
-        for h in range(2):
-            receive(SECOND_AT + 5 + h, z_in2.at[h, 3])
-            final2[unit(y), h * 256 : (h + 1) * 256] = (
-                z_in2[h, 2].astype(F32) + z_in2[h, 3].astype(F32)
-            ).astype(BF16)
-        ref = final2.at[unit(y)]
+            send(SECOND_AT + 11 * h + 5 + k - 1, ref, ref, table, wrap(y + k, 4) * 4 + zh)
+
+    def second_at(x_, h):
+        return pl.ds(pl.multiple_of(x_ * RUN + h * HALF, HALF), HALF)
+
+    def second_turn(h):
+        at = pl.ds(h * HALF, HALF)
+        for k in (1, 3, 2):
+            receive(SECOND_AT + 11 * h + 5 + k - 1, final2.at[unit(wrap(y - k, 4)), at])
         for k in (2, 1, 3):
-            send(SECOND_AT + 7 + k - 1, ref, ref, table, wrap(y + k, 4) * 4 + zh)
-
-    def second_turn():
-        for k in (1, 3, 2):
-            receive(SECOND_AT + 7 + k - 1, final2.at[unit(wrap(y - k, 4))])
-        for k in (2, 1, 3):
-            to_x(SECOND_AT + 10, final2.at[unit(wrap(x + k, 4))], result2.at[:, run_at], k)
-        result2[:, run_at] = final2[unit(x), :]
-
-    def second_collect():
-        for k in (1, 3, 2):
-            at = pl.ds(pl.multiple_of(wrap(x - k, 4) * RUN, RUN), RUN)
-            receive(SECOND_AT + 10 + k - 1, result2.at[:, at])
+            to_x(
+                SECOND_AT + 11 * h + 8,
+                final2.at[unit(wrap(x + k, 4)), at],
+                result2.at[:, second_at(x, h)],
+                k,
+            )
+        result2[:, second_at(x, h)] = final2[unit(x), at]
+
+    def second_collect(h):
+        for k in (1, 3, 2):
+            receive(SECOND_AT + 11 * h + 8 + k - 1, result2.at[:, second_at(wrap(x - k, 4), h)])
 
     def spread_run():
         for k in range(1, 8):
@@ -395,39 +412,39 @@
         lax.fori_loop(0, PEERS, place, 0)
 
     pool_pair(0)
-    gather(0)
     pool_pair(1)
-    gather(1)
-    products(0)
-    gather(2)
-    products(1)
-    first_chunk(0)
-    gather(3)
+    for r in range(CHUNKS):
+        gather(r)
     spread_run()
-    products(2)
-    first_chunk(1)
-    products(3)
+    for r in range(CHUNKS):
+        products(r)
     second_out()
-    first_chunk(2)
+    for r in range(CHUNKS - 1):
+        first_chunk(r)
     first_last()
-    second_exchange()
+    second_exchange(0)
+    second_exchange(1)
     spread_x()
     for p in range(PIECES):
         exchange(p)
-    second_pair()
+    second_pair(0)
+    second_pair(1)
     for p in range(PIECES):
         pair(p)
-    second_finish()
+    second_finish(0)
+    second_finish(1)
     for copy in sent:
         copy.wait_send()
     sent.clear()
     place_pooled()
+    second_turn(0)
     for p in range(PIECES):
         finish(p)
-    second_turn()
+    second_turn(1)
     for p in range(PIECES):
         collect(p)
-    second_collect()
+    second_collect(0)
+    second_collect(1)
     out_first[...] = result[...]
     out_second[...] = result2[...]
     for copy in sent:
@@ -474,7 +491,8 @@
             pltpu.VMEM((LINE, ROWS), BF16),
             pltpu.VMEM((3, HIDDEN, ROWS), BF16),
             pltpu.VMEM((HIDDEN, FEATS), F32),
-            pltpu.VMEM((3, SHARE, FEATS), F32),
+            pltpu.VMEM((HIDDEN, FEATS), BF16),
+            pltpu.VMEM((3, SHARE, FEATS), BF16),
             pltpu.VMEM((PIECES, 4, SHARE, PIECE), BF16),
             pltpu.VMEM((HIDDEN, FEATS), BF16),
             pltpu.VMEM((LINE, RUN), BF16),

time: 65 us -> 63 us (0.969)
  the two profiles are of different devices: /device:TPU:8 before, /device:TPU:32 now
where the time goes in v4:
time: 63 us; the launch traced here: 62.9 us
  Pallas kernels  60 us (95%)
  local copies, waits for them, and re-layouts  2.2 us (3%)
  between operations  0.64 us (1%)
    pallas_call x1, Pallas kernels, shards(): pl.pallas_call(kernel, out_shape=(jax.ShapeDtypeStruct((HIDDEN, FEATS), B...  60 us
    unnamed x3, local copies, waits for them, and re-layouts  2.2 us

profile of v4, /device:TPU:32, one launch (start us, length us, event | category | flops | bytes accessed | tf_op | source)
XLA Modules:
  0.0 62.9 jit_solution(7710842288576712510)
XLA Ops:
  0.6 60.0 %shard_map.112 = (bf16[64,2048]{1,0:T(8,128)(2,1)S(1)}, bf16[64,2048]{1,0:T(8,128)(2,1)S(1)}, bf16[1,8,32768]{2,1,0:T(8,128)(2,1)S(1)}) custom-call(s32[4]{0:T(128)} %widths_hbm.1, bf16[1024,2048]{1,0:T(8,128)(2,1)} %top_hbm.1, bf16[64,1024]{1,0:T(8,128)(2,1)} %cot_hbm.1, bf16[64,2048]{1,0:T(8,128)(2,1)} %first_hbm.1, bf16[64,2048]{1,0:T(8,128)(2,1)} %second_hbm.1, ...), custom_call_target="tpu_custom_call" | custom-call | flops 1073741824 | bytes 8388608 | tf_op jit(solution)/shard_map/pallas_call | solution.py:469
  60.6 0.7 %copy.15 = bf16[64,2048]{1,0:T(8,128)(2,1)} copy(bf16[64,2048]{1,0:T(8,128)(2,1)S(1)} %get-tuple-element.6) | data formatting | bytes 524288
  61.4 0.7 %copy.16 = bf16[64,2048]{1,0:T(8,128)(2,1)} copy(bf16[64,2048]{1,0:T(8,128)(2,1)S(1)} %get-tuple-element.7) | data formatting | bytes 524288
  62.1 0.8 %copy.17 = bf16[1,8,32768]{2,1,0:T(8,128)(2,1)} copy(bf16[1,8,32768]{2,1,0:T(8,128)(2,1)S(1)} %get-tuple-element.8) | data formatting | bytes 1048576

commit v5 on v4

--- a/solution.py
+++ b/solution.py
@@ -14,7 +14,8 @@
 FEATS = 2048
 BLOCK = 64
 RUN = 512
-HALF = RUN // 2
+SLICES = 4
+SLICE = RUN // SLICES
 LINE = 256
 CHUNKS = 4
 CHUNK = ROWS // CHUNKS
@@ -32,7 +33,7 @@
 HIDDEN_AT = WEIGHT_AT + 3
 FIRST_AT = HIDDEN_AT + 3
 SECOND_AT = FIRST_AT + 8 * PIECES
-SPREAD_AT = SECOND_AT + 11 * 2
+SPREAD_AT = SECOND_AT + 11 * SLICES
 COPIES = SPREAD_AT + 7 + 3
 
 
@@ -329,8 +330,8 @@
         )
         y_own2[...] = value
         part2_b[...] = value.astype(BF16)
-        for h in range(2):
-            at = pl.ds(h * HALF, HALF)
+        for h in range(SLICES):
+            at = pl.ds(h * SLICE, SLICE)
             for k in (2, 1, 3):
                 to = wrap(y + k, 4)
                 send(
@@ -342,33 +343,33 @@
                 )
 
     def second_exchange(h):
-        at = pl.ds(h * HALF, HALF)
+        at = pl.ds(h * SLICE, SLICE)
         total = y_own2[unit(y), at]
         for k in (1, 3, 2):
             receive(SECOND_AT + 11 * h + k - 1, y_in2.at[k - 1, :, at])
         for k in range(1, 4):
             total = total + y_in2[k - 1, :, at].astype(F32)
         z_in2[h, 0] = total.astype(BF16)
-        send(SECOND_AT + 11 * h + 3, z_in2.at[h, 0], z_in2.at[h, 1], table, pairs[h])
+        send(SECOND_AT + 11 * h + 3, z_in2.at[h, 0], z_in2.at[h, 1], table, pairs[h % 2])
 
     def second_pair(h):
         receive(SECOND_AT + 11 * h + 3, z_in2.at[h, 1])
         z_in2[h, 2] = (z_in2[h, 0].astype(F32) + z_in2[h, 1].astype(F32)).astype(BF16)
-        send(SECOND_AT + 11 * h + 4, z_in2.at[h, 2], z_in2.at[h, 3], table, pairs[1 - h])
+        send(SECOND_AT + 11 * h + 4, z_in2.at[h, 2], z_in2.at[h, 3], table, pairs[1 - h % 2])
 
     def second_finish(h):
         receive(SECOND_AT + 11 * h + 4, z_in2.at[h, 3])
-        at = pl.ds(h * HALF, HALF)
+        at = pl.ds(h * SLICE, SLICE)
         final2[unit(y), at] = (z_in2[h, 2].astype(F32) + z_in2[h, 3].astype(F32)).astype(BF16)
         ref = final2.at[unit(y), at]
         for k in (2, 1, 3):
             send(SECOND_AT + 11 * h + 5 + k - 1, ref, ref, table, wrap(y + k, 4) * 4 + zh)
 
     def second_at(x_, h):
-        return pl.ds(pl.multiple_of(x_ * RUN + h * HALF, HALF), HALF)
+        return pl.ds(pl.multiple_of(x_ * RUN + h * SLICE, SLICE), SLICE)
 
     def second_turn(h):
-        at = pl.ds(h * HALF, HALF)
+        at = pl.ds(h * SLICE, SLICE)
         for k in (1, 3, 2):
             receive(SECOND_AT + 11 * h + 5 + k - 1, final2.at[unit(wrap(y - k, 4)), at])
         for k in (2, 1, 3):
@@ -422,17 +423,17 @@
     for r in range(CHUNKS - 1):
         first_chunk(r)
     first_last()
-    second_exchange(0)
-    second_exchange(1)
+    for h in range(SLICES):
+        second_exchange(h)
     spread_x()
     for p in range(PIECES):
         exchange(p)
-    second_pair(0)
-    second_pair(1)
+    for h in range(SLICES):
+        second_pair(h)
     for p in range(PIECES):
         pair(p)
-    second_finish(0)
-    second_finish(1)
+    for h in range(SLICES):
+        second_finish(h)
     for copy in sent:
         copy.wait_send()
     sent.clear()
@@ -441,10 +442,12 @@
     for p in range(PIECES):
         finish(p)
     second_turn(1)
+    second_turn(2)
+    second_turn(3)
     for p in range(PIECES):
         collect(p)
-    second_collect(0)
-    second_collect(1)
+    for h in range(SLICES):
+        second_collect(h)
     out_first[...] = result[...]
     out_second[...] = result2[...]
     for copy in sent:
@@ -498,7 +501,7 @@
             pltpu.VMEM((LINE, RUN), BF16),
             pltpu.VMEM((LINE, RUN), F32),
             pltpu.VMEM((3, HIDDEN, RUN), BF16),
-            pltpu.VMEM((2, 4, HIDDEN, RUN // 2), BF16),
+            pltpu.VMEM((4, 4, HIDDEN, SLICE), BF16),
             pltpu.VMEM((LINE, RUN), BF16),
             pltpu.VMEM((HIDDEN, FEATS), BF16),
             pltpu.VMEM((8, 4, 16, 512), BF16),

time: 63 us -> 62.4 us (level)
  no operation moved by 1% of the time
where the time goes in v5:
time: 62.4 us; the launch traced here: 62.3 us
  Pallas kernels  59.5 us (95%)
  local copies, waits for them, and re-layouts  2.2 us (4%)
  between operations  0.64 us (1%)
    pallas_call x1, Pallas kernels, shards(): pl.pallas_call(kernel, out_shape=(jax.ShapeDtypeStruct((HIDDEN, FEATS), B...  59.5 us
    unnamed x3, local copies, waits for them, and re-layouts  2.2 us

profile of v5, /device:TPU:32, one launch (start us, length us, event | category | flops | bytes accessed | tf_op | source)
XLA Modules:
  0.0 62.3 jit_solution(18050018804597326278)
XLA Ops:
  0.6 59.5 %shard_map.112 = (bf16[64,2048]{1,0:T(8,128)(2,1)S(1)}, bf16[64,2048]{1,0:T(8,128)(2,1)S(1)}, bf16[1,8,32768]{2,1,0:T(8,128)(2,1)S(1)}) custom-call(s32[4]{0:T(128)} %widths_hbm.1, bf16[1024,2048]{1,0:T(8,128)(2,1)} %top_hbm.1, bf16[64,1024]{1,0:T(8,128)(2,1)} %cot_hbm.1, bf16[64,2048]{1,0:T(8,128)(2,1)} %first_hbm.1, bf16[64,2048]{1,0:T(8,128)(2,1)} %second_hbm.1, ...), custom_call_target="tpu_custom_call" | custom-call | flops 1073741824 | bytes 8388608 | tf_op jit(solution)/shard_map/pallas_call | solution.py:472
  60.1 0.7 %copy.15 = bf16[64,2048]{1,0:T(8,128)(2,1)} copy(bf16[64,2048]{1,0:T(8,128)(2,1)S(1)} %get-tuple-element.6) | data formatting | bytes 524288
  60.8 0.7 %copy.16 = bf16[64,2048]{1,0:T(8,128)(2,1)} copy(bf16[64,2048]{1,0:T(8,128)(2,1)S(1)} %get-tuple-element.7) | data formatting | bytes 524288
  61.5 0.8 %copy.17 = bf16[1,8,32768]{2,1,0:T(8,128)(2,1)} copy(bf16[1,8,32768]{2,1,0:T(8,128)(2,1)S(1)} %get-tuple-element.8) | data formatting | bytes 1048576

commit v6 on v5

--- a/solution.py
+++ b/solution.py
@@ -249,7 +249,7 @@
         d_hidden[:, at] = value
         d_hidden_b[:, at] = value.astype(BF16)
         at = pl.ds(r * CHUNK, CHUNK)
-        for k in (2, 1, 3):
+        for k in (1, 3, 2):
             to_x(
                 PARTIAL_AT + 3 * r,
                 d_hidden_b.at[unit(wrap(x + k, 4)), at],
@@ -284,7 +284,7 @@
             part[:, at] = value
             part_b[:, at] = value.astype(BF16)
             at = pl.ds(p * PIECE, PIECE)
-            for k in (2, 1, 3):
+            for k in (1, 3, 2):
                 to = wrap(y + k, 4)
                 send(
                     FIRST_AT + 8 * p + k - 1,
@@ -314,7 +314,7 @@
         at = pl.ds(p * PIECE, PIECE)
         result[share(y), at] = (z_in[p, 2].astype(F32) + z_in[p, 3].astype(F32)).astype(BF16)
         ref = result.at[share(y), at]
-        for k in (2, 1, 3):
+        for k in (1, 3, 2):
             send(FIRST_AT + 8 * p + 5 + k - 1, ref, ref, table, wrap(y + k, 4) * 4 + zh)
 
     def collect(p):
@@ -332,7 +332,7 @@
         part2_b[...] = value.astype(BF16)
         for h in range(SLICES):
             at = pl.ds(h * SLICE, SLICE)
-            for k in (2, 1, 3):
+            for k in (1, 3, 2):
                 to = wrap(y + k, 4)
                 send(
                     SECOND_AT + 11 * h + k - 1,
@@ -362,7 +362,7 @@
         at = pl.ds(h * SLICE, SLICE)
         final2[unit(y), at] = (z_in2[h, 2].astype(F32) + z_in2[h, 3].astype(F32)).astype(BF16)
         ref = final2.at[unit(y), at]
-        for k in (2, 1, 3):
+        for k in (1, 3, 2):
             send(SECOND_AT + 11 * h + 5 + k - 1, ref, ref, table, wrap(y + k, 4) * 4 + zh)
 
     def second_at(x_, h):
@@ -372,7 +372,7 @@
         at = pl.ds(h * SLICE, SLICE)
         for k in (1, 3, 2):
             receive(SECOND_AT + 11 * h + 5 + k - 1, final2.at[unit(wrap(y - k, 4)), at])
-        for k in (2, 1, 3):
+        for k in (1, 3, 2):
             to_x(
                 SECOND_AT + 11 * h + 8,
                 final2.at[unit(wrap(x + k, 4)), at],

time: 62.4 us -> 62.8 us (level)
  no operation moved by 1% of the time
where the time goes in v6:
time: 62.8 us; the launch traced here: 62.7 us
  Pallas kernels  59.9 us (95%)
  local copies, waits for them, and re-layouts  2.2 us (4%)
  between operations  0.64 us (1%)
    pallas_call x1, Pallas kernels, shards(): pl.pallas_call(kernel, out_shape=(jax.ShapeDtypeStruct((HIDDEN, FEATS), B...  59.9 us
    unnamed x3, local copies, waits for them, and re-layouts  2.2 us

profile of v6, /device:TPU:32, one launch (start us, length us, event | category | flops | bytes accessed | tf_op | source)
XLA Modules:
  0.0 62.7 jit_solution(15417834177427171081)
XLA Ops:
  0.6 59.9 %shard_map.112 = (bf16[64,2048]{1,0:T(8,128)(2,1)S(1)}, bf16[64,2048]{1,0:T(8,128)(2,1)S(1)}, bf16[1,8,32768]{2,1,0:T(8,128)(2,1)S(1)}) custom-call(s32[4]{0:T(128)} %widths_hbm.1, bf16[1024,2048]{1,0:T(8,128)(2,1)} %top_hbm.1, bf16[64,1024]{1,0:T(8,128)(2,1)} %cot_hbm.1, bf16[64,2048]{1,0:T(8,128)(2,1)} %first_hbm.1, bf16[64,2048]{1,0:T(8,128)(2,1)} %second_hbm.1, ...), custom_call_target="tpu_custom_call" | custom-call | flops 1073741824 | bytes 8388608 | tf_op jit(solution)/shard_map/pallas_call | solution.py:472
  60.5 0.7 %copy.15 = bf16[64,2048]{1,0:T(8,128)(2,1)} copy(bf16[64,2048]{1,0:T(8,128)(2,1)S(1)} %get-tuple-element.6) | data formatting | bytes 524288
  61.2 0.7 %copy.16 = bf16[64,2048]{1,0:T(8,128)(2,1)} copy(bf16[64,2048]{1,0:T(8,128)(2,1)S(1)} %get-tuple-element.7) | data formatting | bytes 524288
  61.9 0.8 %copy.17 = bf16[1,8,32768]{2,1,0:T(8,128)(2,1)} copy(bf16[1,8,32768]{2,1,0:T(8,128)(2,1)S(1)} %get-tuple-element.8) | data formatting | bytes 1048576
